TPU v7x, 32 devices: a whole 2x2x4 slice. The times are simulated.
32 devices in a mesh: gx: 8 (over y, x, core), gy: 4 (over z).
Axes of the slice: x: 2, y: 2, z: 4, core: 2. Of those that a mesh axis runs over, the one named last changes fastest.
Arguments:
- fine_now: float32 [3, 64, 64, 128], P(None, 'gx', 'gy'), may hold values from -6 to 6
- fine_prev: float32 [3, 64, 64, 128], P(None, 'gx', 'gy'), may hold values from -6 to 6
- coarse_now: float32 [3, 32, 32, 128], P(None, 'gx', 'gy'), may hold values from -6 to 6
- coarse_prev: float32 [3, 32, 32, 128], P(None, 'gx', 'gy'), may hold values from -6 to 6
- fine_rho: float32 [64, 64, 128], P('gx', 'gy'), may hold values from 1 to 3
- fine_mu: float32 [64, 64, 128], P('gx', 'gy'), may hold values from 0.3 to 1.5
- fine_lam: float32 [64, 64, 128], P('gx', 'gy'), may hold values from 0.3 to 1.5
- fine_metric: float32 [64, 64, 128], P('gx', 'gy'), may hold values from 0.5 to 2
- coarse_rho: float32 [32, 32, 128], P('gx', 'gy'), may hold values from 1 to 3
- coarse_mu: float32 [32, 32, 128], P('gx', 'gy'), may hold values from 0.3 to 1.5
- coarse_lam: float32 [32, 32, 128], P('gx', 'gy'), may hold values from 0.3 to 1.5
- coarse_metric: float32 [32, 32, 128], P('gx', 'gy'), may hold values from 0.5 to 2
- couple_index: int32 [64, 64, 16], P('gx', 'gy'), may hold values from 0 to 95, as said below
- couple_weight: float32 [64, 64, 16], P('gx', 'gy'), may hold values from 0 to 0.125
Outputs:
- fine_field: float32 [3, 64, 64, 128], P(None, 'gx', 'gy')
- coarse_field: float32 [3, 32, 32, 128], P(None, 'gx', 'gy')
Inputs may be any that keep to these rules, and one draw needn't show every extreme that they name: `couple_index`: the sixteen indices of a fine point are a 4 x 4 patch of neighbouring coarse cells of its block's widened top plane, lying within 2 coarse cells of the point's own coarse cell.
All inputs are finite; a program needn't handle non-finite values.
Results may differ from a plain program's by a relative error of at most 0.0001.
Values sent between devices are 32-bit elements; how exact they have to be, the bound alone decides.
A program may use at most 64 MiB of HBM per device.

v0:
```python
import functools

import jax
import jax.numpy as jnp
from jax import lax
from jax.experimental import pallas as pl
from jax.experimental.pallas import tpu as pltpu
from jax.sharding import PartitionSpec as P

MESH = pl.DeviceIdType.MESH
f32 = jnp.float32
bf16 = jnp.bfloat16
time_step = 0.25
OFF = 8
SIDES = ((-1, 0), (1, 0), (0, -1), (0, 1))
CORNERS = ((-1, -1), (-1, 1), (1, -1), (1, 1))
DIRS = SIDES + CORNERS


def vertical_table12(layers):
    level_in = lax.broadcasted_iota(jnp.int32, (layers, layers), 0)
    level_out = lax.broadcasted_iota(jnp.int32, (layers, layers), 1)
    apart = level_in - level_out
    table = jnp.where(apart == -2, 1.0, 0.0)
    table = jnp.where(apart == -1, -8.0, table)
    table = jnp.where(apart == 1, 8.0, table)
    table = jnp.where(apart == 2, -1.0, table)
    last = layers - 1
    edges = {
        0: ((0, -18.0), (1, 24.0), (2, -6.0)),
        1: ((0, -6.0), (2, 6.0)),
        last - 1: ((last - 2, -6.0), (last, 6.0)),
        last: ((last - 2, 6.0), (last - 1, -24.0), (last, 18.0)),
    }
    for row, taps in edges.items():
        column = jnp.zeros_like(table)
        for level, value in taps:
            column = jnp.where(level_in == level, value, column)
        table = jnp.where(level_out == row, column, table)
    return table.astype(bf16)


def halves(values):
    high = values.astype(bf16)
    low = (values - high.astype(f32)).astype(bf16)
    return high, low


def dot(left, right):
    return jnp.dot(left, right, preferred_element_type=f32)


def vertical12(values, table2):
    shape = values.shape
    high, low = halves(values.reshape(-1, shape[-1]))
    return dot(jnp.concatenate([high, low], axis=1), table2).reshape(shape)


def before_halo(u, metric, lift, base, earlier, shear, table2, nx, ny):
    inner_x, inner_y = slice(2, 2 + nx), slice(OFF, OFF + ny)
    metric_in = metric[inner_x, inner_y] * (1.0 / 12.0)
    present = u[0:3, inner_x, inner_y]
    slopes = metric_in * vertical12(present, table2)
    lift[inner_x, inner_y] = slopes[2]
    bent = metric_in * vertical12(slopes, table2)
    for c in range(3):
        base[c] = 2.0 * present[c] - earlier(c) + shear * bent[c]


def after_halo(u, metric, lift, bend, base, shear, both, table2, nx, ny, spacing, put):
    inner_x, inner_y = slice(2, 2 + nx), slice(OFF, OFF + ny)
    t1 = 1.0 / (12.0 * spacing)
    t2 = 1.0 / (12.0 * spacing * spacing)

    def first(m2, m1, p1, p2):
        return t1 * ((m2 - p2) + 8.0 * (p1 - m1))

    def second(m2, m1, mid, p1, p2):
        return t2 * (16.0 * (m1 + p1) - (m2 + p2) - 30.0 * mid)

    def along_y(read):
        return [read(slice(OFF + s, OFF + s + ny)) for s in (-2, -1, 0, 1, 2)]

    def along_x(values):
        return [values[2 + s : 2 + s + nx] for s in (-2, -1, 0, 1, 2)]

    layers = u.shape[-1]
    rims = (
        (slice(0, 2), inner_y),
        (slice(2 + nx, 4 + nx), inner_y),
        (inner_x, slice(0, OFF)),
        (inner_x, slice(OFF + ny, 2 * OFF + ny)),
    )
    rows = [u[2, xs, ys].reshape(-1, layers) for xs, ys in rims]
    found = vertical12(jnp.concatenate(rows, axis=0), table2)
    start = 0
    for (xs, ys), part in zip(rims, rows):
        scale = metric[xs, ys] * (1.0 / 12.0)
        lift[xs, ys] = scale * found[start : start + part.shape[0]].reshape(scale.shape)
        start += part.shape[0]

    m2, m1, mid, p1, p2 = along_x(u[0])
    bend[...] = first(m2, m1, p1, p2) + lift[inner_x]
    curve_x0 = second(*[v[:, inner_y] for v in (m2, m1, mid, p1, p2)])
    slope_x0 = bend[:, inner_y]

    m2, m1, mid, p1, p2 = along_y(lambda ys: u[1, :, ys])
    slant = first(m2, m1, p1, p2) + lift[:, inner_y]
    spread = slant[inner_x] + slope_x0 - lift[inner_x, inner_y]
    bent = (metric[inner_x, inner_y] * (1.0 / 12.0)) * vertical12(spread, table2)
    curve_y1 = second(*[v[inner_x] for v in (m2, m1, mid, p1, p2)])
    curve_x1 = second(*along_x(mid))
    m2, m1, _, p1, p2 = along_x(slant)
    graddiv_0 = curve_x0 + first(m2, m1, p1, p2)
    curve_y0 = second(*along_y(lambda ys: u[0, inner_x, ys]))
    put(0, base[0] + shear * (curve_x0 + curve_y0) + both * graddiv_0)

    m2, m1, mid, p1, p2 = along_y(lambda ys: bend[:, ys])
    graddiv_1 = curve_y1 + first(m2, m1, p1, p2)
    put(1, base[1] + shear * (curve_x1 + curve_y1) + both * graddiv_1)

    curve_2 = second(*along_x(u[2, :, inner_y])) + second(*along_y(lambda ys: u[2, inner_x, ys]))
    put(2, base[2] + shear * curve_2 + both * bent)


def kernel(
    size_x,
    size_y,
    fine_now,
    fine_prev,
    coarse_now,
    coarse_prev,
    fine_rho,
    fine_mu,
    fine_lam,
    fine_metric,
    coarse_rho,
    coarse_mu,
    coarse_lam,
    coarse_metric,
    couple_index,
    couple_weight,
    fine_out,
    coarse_out,
    f1,
    f2,
    c1,
    c2,
    f_old,
    c_old,
    f_par,
    c_par,
    index_in,
    weight_in,
    f_lift,
    f_bend,
    c_lift,
    c_bend,
    t2,
    mix,
    table,
    f_base,
    c_base,
    f_last,
    c_last,
    load_sem,
    out_sem,
    send_sem,
    recv_sem,
):
    nxf, nyf, layers = fine_rho.shape
    nxc, nyc, _ = coarse_rho.shape
    span = OFF + nyc
    gx, gy = lax.axis_index("gx"), lax.axis_index("gy")

    def inner(nx, ny):
        return pl.ds(2, nx), pl.ds(OFF, ny)

    def exists(dx, dy):
        ok = None
        for step, position, size in ((dx, gx, size_x), (dy, gy, size_y)):
            if step:
                here = position >= 1 if step < 0 else position <= size - 2
                ok = here if ok is None else jnp.logical_and(ok, here)
        return ok

    barrier = pltpu.get_barrier_semaphore()
    for dx, dy in DIRS:

        @pl.when(exists(dx, dy))
        def _():
            pl.semaphore_signal(
                barrier, inc=1, device_id=(gx + dx, gy + dy), device_id_type=MESH
            )

    fx, fy = inner(nxf, nyf)
    cx, cy = inner(nxc, nyc)
    pairs = [
        (coarse_now, c1.at[0:3, cx, cy]),
        (coarse_metric, c1.at[3, cx, cy]),
        (fine_now, f1.at[0:3, fx, fy]),
        (fine_metric, f1.at[3, fx, fy]),
        (coarse_rho, c_par.at[0]),
        (coarse_mu, c_par.at[1]),
        (coarse_lam, c_par.at[2]),
        (coarse_prev, c_old),
        (fine_rho, f_par.at[0]),
        (fine_mu, f_par.at[1]),
        (fine_lam, f_par.at[2]),
        (fine_prev, f_old),
        (couple_index, index_in),
        (couple_weight, weight_in),
    ]
    loads = [
        pltpu.make_async_copy(source, target, load_sem.at[n])
        for n, (source, target) in enumerate(pairs)
    ]
    for load in loads:
        load.start()

    half = vertical_table12(layers)
    table[...] = jnp.concatenate([half, half], axis=0)

    def source_range(step, start, length):
        return {-1: pl.ds(start, 2), 1: pl.ds(start + length - 2, 2), 0: pl.ds(start, length)}[step]

    def target_range(step, start, length, wrap=0):
        after = start + length - wrap
        return {-1: pl.ds(after, 2), 1: pl.ds(start - 2, 2), 0: pl.ds(start, length)}[step]

    class Exchange:
        def __init__(self, base, buffer, nx, ny, sides, corners, wrap=0):
            self.copies = []
            self.targets = []
            for n, (dx, dy) in enumerate(DIRS):
                parts = sides if n < 4 else corners
                xs, ys = source_range(dx, 2, nx), source_range(dy, OFF, ny)
                xt, yt = target_range(dx, 2, nx), target_range(dy, OFF, ny, wrap)
                if parts is None:
                    src, dst = buffer.at[xs, ys], buffer.at[xt, yt]
                    self.targets.append((buffer, (xt, yt), (xt.size, yt.size, layers)))
                else:
                    ps = pl.ds(0, parts)
                    src, dst = buffer.at[ps, xs, ys], buffer.at[ps, xt, yt]
                    self.targets.append((buffer, (ps, xt, yt), (parts, xt.size, yt.size, layers)))
                copy = pltpu.make_async_remote_copy(
                    src_ref=src,
                    dst_ref=dst,
                    send_sem=send_sem.at[base + n],
                    recv_sem=recv_sem.at[base + n],
                    device_id=(gx + dx, gy + dy),
                    device_id_type=MESH,
                )
                self.copies.append(copy)

        def start(self):
            for (dx, dy), copy in zip(DIRS, self.copies):
                pl.when(exists(dx, dy))(copy.start)

        def arrive(self):
            for (dx, dy), copy in zip(DIRS, self.copies):
                pl.when(exists(-dx, -dy))(copy.wait_recv)

        def finish(self):
            for (dx, dy), copy in zip(DIRS, self.copies):
                pl.when(exists(dx, dy))(copy.wait_send)

    coarse_a = Exchange(0, c1, nxc, nyc, 4, 2)
    fine_a = Exchange(8, f1, nxf, nyf, 4, 2)
    coarse_b = Exchange(16, c2, nxc, nyc, 3, 3)
    fine_b = Exchange(24, f2, nxf, nyf, 3, 2)
    top_c = Exchange(32, t2, nxc, nyc, None, None, wrap=span)
    exchanges = (coarse_a, fine_a, coarse_b, fine_b, top_c)

    for load in loads[0:4]:
        load.wait()
    sides_x = 1 + (gx >= 1).astype(jnp.int32) + (gx <= size_x - 2).astype(jnp.int32)
    sides_y = 1 + (gy >= 1).astype(jnp.int32) + (gy <= size_y - 2).astype(jnp.int32)
    pl.semaphore_wait(barrier, sides_x * sides_y - 1)
    coarse_a.start()
    fine_a.start()

    for n, (dx, dy) in enumerate(DIRS):

        @pl.when(jnp.logical_not(exists(-dx, -dy)))
        def _():
            for exchange in exchanges:
                buffer, where, shape = exchange.targets[n]
                buffer[where] = jnp.zeros(shape, f32)

    cells = (nxc + 4) * span

    def build_mix():
        width = nyc + 4
        reciprocal = (2048 + width - 1) // width
        index = index_in[...].reshape(nxf * nyf, -1)
        weight = weight_in[...].reshape(nxf * nyf, -1)
        row = jnp.right_shift(index * reciprocal, 11)
        column = index - row * width + (OFF - 2)
        column = jnp.where(column >= span, column - span, column)
        place = row * span + column
        cell = lax.broadcasted_iota(jnp.int32, (nxf * nyf, cells), 1)
        total = jnp.zeros((nxf * nyf, cells), f32)
        for j in range(index.shape[1]):
            total += jnp.where(cell == place[:, j : j + 1], weight[:, j : j + 1], 0.0)
        mix_high, mix_low = halves(total)
        mix[0] = mix_high
        mix[1] = mix_low

    lane = lax.broadcasted_iota(jnp.int32, (1, 1, layers), 2)

    def tops(parts):
        out = None
        for c, values in enumerate(parts):
            only = jnp.where(lane == layers - 1, values, 0.0)
            moved = pltpu.roll(only.reshape(-1, layers), c + 1, 1).reshape(values.shape)
            out = moved if out is None else out + moved
        return out

    def interface(top, parts):
        high, low = halves(top.reshape(cells, layers))
        found = dot(mix[0], high) + (dot(mix[1], high) + dot(mix[0], low))
        result = []
        for c, values in enumerate(parts):
            moved = found if c == 0 else pltpu.roll(found, layers - c, 1)
            result.append(jnp.where(lane == 0, moved.reshape(values.shape), values))
        return result

    f_in = (slice(2, 2 + nxf), slice(OFF, OFF + nyf))
    c_in = (slice(2, 2 + nxc), slice(OFF, OFF + nyc))

    def parameters(par):
        scale = (time_step * time_step) / par[0]
        shear = par[1]
        par[0] = shear * scale
        par[1] = (par[2] + shear) * scale

    def fine_before(u, earlier):
        before_halo(u, f1.at[3], f_lift, f_base, earlier, f_par[0], table[...], nxf, nyf)

    def coarse_before(u, earlier):
        before_halo(u, c1.at[3], c_lift, c_base, earlier, c_par[0], table[...], nxc, nyc)

    def fine_after(u, put):
        after_halo(
            u, f1.at[3], f_lift, f_bend, f_base, f_par[0], f_par[1], table[...], nxf, nyf, 1.0, put
        )

    def coarse_after(u, put):
        after_halo(
            u, c1.at[3], c_lift, c_bend, c_base, c_par[0], c_par[1], table[...], nxc, nyc, 2.0, put
        )

    def put_in(buffer, where):
        def put(c, values):
            buffer[c, where[0], where[1]] = values

        return put

    def put_out(buffer):
        def put(c, values):
            buffer[c] = values

        return put

    for load in loads[4:8]:
        load.wait()
    parameters(c_par)
    coarse_before(c1, lambda c: c_old[c])
    coarse_a.arrive()
    coarse_after(c1, put_in(c2, c_in))
    coarse_b.start()
    for load in loads[8:12]:
        load.wait()
    parameters(f_par)
    fine_before(f1, lambda c: f_old[c])
    for load in loads[12:]:
        load.wait()
    build_mix()
    fine_a.arrive()
    fine_after(f1, put_in(f2, f_in))
    coarse_b.arrive()
    sub = lax.broadcasted_iota(jnp.int32, (1, OFF, 1), 1)
    rims = []
    for c in range(3):
        after, before = c2[c, :, OFF + nyc : 2 * OFF + nyc], c2[c, :, 0:OFF]
        rims.append(jnp.where(sub < 2, after, jnp.where(sub >= OFF - 2, before, 0.0)))
    top = jnp.concatenate([tops(rims), tops([c2[c, :, c_in[1]] for c in range(3)])], axis=1)
    for c, values in enumerate(interface(top, [f2[c, f_in[0], f_in[1]] for c in range(3)])):
        f2[c, f_in[0], f_in[1]] = values
    fine_b.start()

    coarse_before(c2, lambda c: c1[c, c_in[0], c_in[1]])
    coarse_after(c2, put_out(c_last))
    t2[c_in[0], c_in[1]] = tops([c_last[c] for c in range(3)])
    top_c.start()
    store_coarse = pltpu.make_async_copy(c_last, coarse_out, out_sem.at[0])
    store_coarse.start()
    fine_before(f2, lambda c: f1[c, f_in[0], f_in[1]])
    fine_b.arrive()
    fine_after(f2, put_out(f_last))
    top_c.arrive()
    rim = jnp.where(jnp.logical_or(sub < 2, sub >= OFF - 2), t2[:, 0:OFF], 0.0)
    top = jnp.concatenate([rim, t2[:, OFF:span]], axis=1)
    for c, values in enumerate(interface(top, [f_last[c] for c in range(3)])):
        f_last[c] = values
    store_fine = pltpu.make_async_copy(f_last, fine_out, out_sem.at[1])
    store_fine.start()
    for exchange in exchanges:
        exchange.finish()
    store_coarse.wait()
    store_fine.wait()


def finish(fine_in, coarse_in, fine_out, coarse_out, sem):
    copies = [
        pltpu.make_async_copy(fine_in, fine_out, sem.at[0]),
        pltpu.make_async_copy(coarse_in, coarse_out, sem.at[1]),
    ]
    for copy in copies:
        copy.start()
    for copy in copies:
        copy.wait()


def solution(mesh):
    size_x, size_y = mesh.shape["gx"], mesh.shape["gy"]

    def on_device(*args):
        fine, coarse = args[0], args[2]
        _, nxf, nyf, layers = fine.shape
        _, nxc, nyc, _ = coarse.shape
        index = args[12]

        def wide(parts, nx, ny):
            return pltpu.VMEM((parts, nx + 4, ny + 2 * OFF, layers), f32)

        span = OFF + nyc
        scratch = [
            wide(4, nxf, nyf),
            wide(3, nxf, nyf),
            wide(4, nxc, nyc),
            wide(3, nxc, nyc),
            pltpu.VMEM(fine.shape, f32),
            pltpu.VMEM(coarse.shape, f32),
            pltpu.VMEM(fine.shape, f32),
            pltpu.VMEM(coarse.shape, f32),
            pltpu.VMEM(index.shape, jnp.int32),
            pltpu.VMEM(index.shape, f32),
            pltpu.VMEM((nxf + 4, nyf + 2 * OFF, layers), f32),
            pltpu.VMEM((nxf, nyf + 2 * OFF, layers), f32),
            pltpu.VMEM((nxc + 4, nyc + 2 * OFF, layers), f32),
            pltpu.VMEM((nxc, nyc + 2 * OFF, layers), f32),
            pltpu.VMEM((nxc + 4, span, layers), f32),
            pltpu.VMEM((2, nxf * nyf, (nxc + 4) * span), bf16),
            pltpu.VMEM((2 * layers, layers), bf16),
            pltpu.VMEM(fine.shape, f32),
            pltpu.VMEM(coarse.shape, f32),
            pltpu.VMEM(fine.shape, f32),
            pltpu.VMEM(coarse.shape, f32),
            pltpu.SemaphoreType.DMA((14,)),
            pltpu.SemaphoreType.DMA((2,)),
            pltpu.SemaphoreType.DMA((40,)),
            pltpu.SemaphoreType.DMA((40,)),
        ]
        shapes = (
            jax.ShapeDtypeStruct(fine.shape, f32),
            jax.ShapeDtypeStruct(coarse.shape, f32),
        )
        hbm = pl.BlockSpec(memory_space=pltpu.HBM)
        results = pl.pallas_call(
            functools.partial(kernel, size_x, size_y),
            out_shape=shapes,
            in_specs=[hbm] * 14,
            out_specs=(hbm, hbm),
            scratch_shapes=scratch,
            compiler_params=pltpu.CompilerParams(
                collective_id=0, has_side_effects=True, vmem_limit_bytes=56 * 1024 * 1024
            ),
        )(*args)
        return pl.pallas_call(
            finish,
            out_shape=shapes,
            in_specs=[hbm, hbm],
            out_specs=(hbm, hbm),
            scratch_shapes=[pltpu.SemaphoreType.DMA((2,))],
            compiler_params=pltpu.CompilerParams(vmem_limit_bytes=56 * 1024 * 1024),
        )(*results)

    field, flat = P(None, "gx", "gy", None), P("gx", "gy", None)
    return jax.shard_map(
        on_device,
        mesh=mesh,
        in_specs=(field,) * 4 + (flat,) * 10,
        out_specs=(field, field),
        check_vma=False,
    )
```

profile of v0, /device:TPU:3, one launch (start us, length us, event | category | flops | bytes accessed | tf_op | source)
XLA Modules:
  0.0 25.6 jit_solution(2072664372947726303)
XLA Ops:
  0.6 16.4 %shard_map.149 = (f32[3,8,16,128]{3,2,1,0:T(8,128)}, f32[3,4,8,128]{3,2,1,0:T(8,128)}) custom-call(f32[3,8,16,128]{3,2,1,0:T(8,128)} %fine_now.1, f32[3,8,16,128]{3,2,1,0:T(8,128)} %fine_prev.1, f32[3,4,8,128]{3,2,1,0:T(8,128)} %coarse_now.1, f32[3,4,8,128]{3,2,1,0:T(8,128)} %coarse_prev.1, f32[8,16,128]{2,1,0:T(8,128)} %fine_rho.1, f32[8,16,128]{2,1,0:T(8,128)} %fine_mu.1, ...), custom_call_target="tpu_custom_call" | custom-call | tf_op jit(solution)/shard_map/pallas_call | solution.py:471
  17.0 8.6 %shard_map.150 = (f32[3,8,16,128]{3,2,1,0:T(8,128)}, f32[3,4,8,128]{3,2,1,0:T(8,128)}) custom-call(f32[3,8,16,128]{3,2,1,0:T(8,128)} %get-tuple-element.4.fine_in, f32[3,4,8,128]{3,2,1,0:T(8,128)} %get-tuple-element.5.coarse_in), custom_call_target="tpu_custom_call" | custom-call | tf_op jit(solution)/shard_map/pallas_call | solution.py:481
where the time goes:
time: 25.7 us; the launch traced here: 25.6 us
  Pallas kernels  24.9 us (97%)
  between operations  0.64 us (2%)
    pallas_call x1, Pallas kernels, on_device(): pl.pallas_call(functools.partial(kernel, size_x, size_y), out_shape=shape...  16.4 us
    pallas_call x1, Pallas kernels, on_device(): pl.pallas_call(finish, out_shape=shapes, in_specs=[hbm, hbm], out_specs=(...  8.57 us

commit v1 on v0

--- a/solution.py
+++ b/solution.py
@@ -161,10 +161,7 @@
     table,
     f_base,
     c_base,
-    f_last,
-    c_last,
     load_sem,
-    out_sem,
     send_sem,
     recv_sem,
 ):
@@ -254,8 +251,8 @@
                 self.copies.append(copy)
 
         def start(self):
-            for (dx, dy), copy in zip(DIRS, self.copies):
-                pl.when(exists(dx, dy))(copy.start)
+            for n in (4, 5, 6, 7, 0, 1, 2, 3):
+                pl.when(exists(*DIRS[n]))(self.copies[n].start)
 
         def arrive(self):
             for (dx, dy), copy in zip(DIRS, self.copies):
@@ -391,25 +388,19 @@
     fine_b.start()
 
     coarse_before(c2, lambda c: c1[c, c_in[0], c_in[1]])
-    coarse_after(c2, put_out(c_last))
-    t2[c_in[0], c_in[1]] = tops([c_last[c] for c in range(3)])
+    coarse_after(c2, put_out(coarse_out))
+    t2[c_in[0], c_in[1]] = tops([coarse_out[c] for c in range(3)])
     top_c.start()
-    store_coarse = pltpu.make_async_copy(c_last, coarse_out, out_sem.at[0])
-    store_coarse.start()
     fine_before(f2, lambda c: f1[c, f_in[0], f_in[1]])
     fine_b.arrive()
-    fine_after(f2, put_out(f_last))
+    fine_after(f2, put_out(fine_out))
     top_c.arrive()
     rim = jnp.where(jnp.logical_or(sub < 2, sub >= OFF - 2), t2[:, 0:OFF], 0.0)
     top = jnp.concatenate([rim, t2[:, OFF:span]], axis=1)
-    for c, values in enumerate(interface(top, [f_last[c] for c in range(3)])):
-        f_last[c] = values
-    store_fine = pltpu.make_async_copy(f_last, fine_out, out_sem.at[1])
-    store_fine.start()
+    for c, values in enumerate(interface(top, [fine_out[c] for c in range(3)])):
+        fine_out[c] = values
     for exchange in exchanges:
         exchange.finish()
-    store_coarse.wait()
-    store_fine.wait()
 
 
 def finish(fine_in, coarse_in, fine_out, coarse_out, sem):
@@ -456,10 +447,7 @@
             pltpu.VMEM((2 * layers, layers), bf16),
             pltpu.VMEM(fine.shape, f32),
             pltpu.VMEM(coarse.shape, f32),
-            pltpu.VMEM(fine.shape, f32),
-            pltpu.VMEM(coarse.shape, f32),
             pltpu.SemaphoreType.DMA((14,)),
-            pltpu.SemaphoreType.DMA((2,)),
             pltpu.SemaphoreType.DMA((40,)),
             pltpu.SemaphoreType.DMA((40,)),
         ]
@@ -467,24 +455,25 @@
             jax.ShapeDtypeStruct(fine.shape, f32),
             jax.ShapeDtypeStruct(coarse.shape, f32),
         )
-        hbm = pl.BlockSpec(memory_space=pltpu.HBM)
+        hbm, vmem = pl.BlockSpec(memory_space=pltpu.HBM), pl.BlockSpec(memory_space=pltpu.VMEM)
+        args = [pltpu.with_memory_space_constraint(arg, pltpu.HBM) for arg in args]
         results = pl.pallas_call(
             functools.partial(kernel, size_x, size_y),
-            out_shape=shapes,
+            out_shape=(pltpu.VMEM(fine.shape, f32), pltpu.VMEM(coarse.shape, f32)),
             in_specs=[hbm] * 14,
-            out_specs=(hbm, hbm),
+            out_specs=(vmem, vmem),
             scratch_shapes=scratch,
             compiler_params=pltpu.CompilerParams(
-                collective_id=0, has_side_effects=True, vmem_limit_bytes=56 * 1024 * 1024
+                collective_id=0, has_side_effects=True, vmem_limit_bytes=32 * 1024 * 1024
             ),
         )(*args)
         return pl.pallas_call(
             finish,
             out_shape=shapes,
-            in_specs=[hbm, hbm],
+            in_specs=[vmem, vmem],
             out_specs=(hbm, hbm),
             scratch_shapes=[pltpu.SemaphoreType.DMA((2,))],
-            compiler_params=pltpu.CompilerParams(vmem_limit_bytes=56 * 1024 * 1024),
+            compiler_params=pltpu.CompilerParams(vmem_limit_bytes=16 * 1024 * 1024),
         )(*results)
 
     field, flat = P(None, "gx", "gy", None), P("gx", "gy", None)

time: 25.7 us -> 17 us (0.66)
  Pallas kernels: 24.9 us -> 16.2 us
    pallas_call x2, Pallas kernels: 24.9 us -> 16.2 us  [the longest x1 15.5 us: on_device(): pl.pallas_call(functools.partial(kernel, size_x, size_y), out_shape=(pltp...]
where the time goes in v1:
time: 17 us; the launch traced here: 16.8 us
  Pallas kernels  16.2 us (95%)
  between operations  0.64 us (4%)
    pallas_call x1, Pallas kernels, on_device(): pl.pallas_call(functools.partial(kernel, size_x, size_y), out_shape=(pltp...  15.5 us
    pallas_call x1, Pallas kernels, on_device(): pl.pallas_call(finish, out_shape=shapes, in_specs=[vmem, vmem], out_specs...  0.7 us

profile of v1, /device:TPU:3, one launch (start us, length us, event | category | flops | bytes accessed | tf_op | source)
XLA Modules:
  0.0 16.8 jit_solution(5532262506338101934)
XLA Ops:
  0.6 15.5 %shard_map.149 = (f32[3,8,16,128]{3,2,1,0:T(8,128)S(1)}, f32[3,4,8,128]{3,2,1,0:T(8,128)S(1)}) custom-call(f32[3,8,16,128]{3,2,1,0:T(8,128)} %fine_now.1, f32[3,8,16,128]{3,2,1,0:T(8,128)} %fine_prev.1, f32[3,4,8,128]{3,2,1,0:T(8,128)} %coarse_now.1, f32[3,4,8,128]{3,2,1,0:T(8,128)} %coarse_prev.1, f32[8,16,128]{2,1,0:T(8,128)} %fine_rho.1, ...), custom_call_target="tpu_custom_call" | custom-call | tf_op jit(solution)/shard_map/pallas_call | solution.py:460
  16.1 0.7 %shard_map.150 = (f32[3,8,16,128]{3,2,1,0:T(8,128)}, f32[3,4,8,128]{3,2,1,0:T(8,128)}) custom-call(f32[3,8,16,128]{3,2,1,0:T(8,128)S(1)} %get-tuple-element.4.fine_in, f32[3,4,8,128]{3,2,1,0:T(8,128)S(1)} %get-tuple-element.5.coarse_in), custom_call_target="tpu_custom_call" | custom-call | tf_op jit(solution)/shard_map/pallas_call | solution.py:470

commit v2 on v1

--- a/solution.py
+++ b/solution.py
@@ -142,12 +142,8 @@
     couple_weight,
     fine_out,
     coarse_out,
-    f1,
-    f2,
-    c1,
-    c2,
-    f_old,
-    c_old,
+    f_all,
+    c_all,
     f_par,
     c_par,
     index_in,
@@ -156,7 +152,6 @@
     f_bend,
     c_lift,
     c_bend,
-    t2,
     mix,
     table,
     f_base,
@@ -193,18 +188,18 @@
     fx, fy = inner(nxf, nyf)
     cx, cy = inner(nxc, nyc)
     pairs = [
-        (coarse_now, c1.at[0:3, cx, cy]),
-        (coarse_metric, c1.at[3, cx, cy]),
-        (fine_now, f1.at[0:3, fx, fy]),
-        (fine_metric, f1.at[3, fx, fy]),
+        (coarse_now, c_all.at[1, 0:3, cx, cy]),
+        (coarse_metric, c_all.at[1, 3, cx, cy]),
+        (fine_now, f_all.at[1, 0:3, fx, fy]),
+        (fine_metric, f_all.at[1, 3, fx, fy]),
         (coarse_rho, c_par.at[0]),
         (coarse_mu, c_par.at[1]),
         (coarse_lam, c_par.at[2]),
-        (coarse_prev, c_old),
+        (coarse_prev, c_all.at[0, 0:3, cx, cy]),
         (fine_rho, f_par.at[0]),
         (fine_mu, f_par.at[1]),
         (fine_lam, f_par.at[2]),
-        (fine_prev, f_old),
+        (fine_prev, f_all.at[0, 0:3, fx, fy]),
         (couple_index, index_in),
         (couple_weight, weight_in),
     ]
@@ -221,28 +216,23 @@
     def source_range(step, start, length):
         return {-1: pl.ds(start, 2), 1: pl.ds(start + length - 2, 2), 0: pl.ds(start, length)}[step]
 
-    def target_range(step, start, length, wrap=0):
-        after = start + length - wrap
-        return {-1: pl.ds(after, 2), 1: pl.ds(start - 2, 2), 0: pl.ds(start, length)}[step]
+    def target_range(step, start, length):
+        return {-1: pl.ds(start + length, 2), 1: pl.ds(start - 2, 2), 0: pl.ds(start, length)}[step]
 
     class Exchange:
-        def __init__(self, base, buffer, nx, ny, sides, corners, wrap=0):
+        def __init__(self, base, buffer, slot, nx, ny, sides, corners):
+            self.buffer, self.slot = buffer, slot
             self.copies = []
             self.targets = []
             for n, (dx, dy) in enumerate(DIRS):
                 parts = sides if n < 4 else corners
                 xs, ys = source_range(dx, 2, nx), source_range(dy, OFF, ny)
-                xt, yt = target_range(dx, 2, nx), target_range(dy, OFF, ny, wrap)
-                if parts is None:
-                    src, dst = buffer.at[xs, ys], buffer.at[xt, yt]
-                    self.targets.append((buffer, (xt, yt), (xt.size, yt.size, layers)))
-                else:
-                    ps = pl.ds(0, parts)
-                    src, dst = buffer.at[ps, xs, ys], buffer.at[ps, xt, yt]
-                    self.targets.append((buffer, (ps, xt, yt), (parts, xt.size, yt.size, layers)))
+                xt, yt = target_range(dx, 2, nx), target_range(dy, OFF, ny)
+                ps = pl.ds(0, parts)
+                self.targets.append(((slot, ps, xt, yt), (parts, xt.size, yt.size, layers)))
                 copy = pltpu.make_async_remote_copy(
-                    src_ref=src,
-                    dst_ref=dst,
+                    src_ref=buffer.at[slot, ps, xs, ys],
+                    dst_ref=buffer.at[slot, ps, xt, yt],
                     send_sem=send_sem.at[base + n],
                     recv_sem=recv_sem.at[base + n],
                     device_id=(gx + dx, gy + dy),
@@ -262,12 +252,13 @@
             for (dx, dy), copy in zip(DIRS, self.copies):
                 pl.when(exists(dx, dy))(copy.wait_send)
 
-    coarse_a = Exchange(0, c1, nxc, nyc, 4, 2)
-    fine_a = Exchange(8, f1, nxf, nyf, 4, 2)
-    coarse_b = Exchange(16, c2, nxc, nyc, 3, 3)
-    fine_b = Exchange(24, f2, nxf, nyf, 3, 2)
-    top_c = Exchange(32, t2, nxc, nyc, None, None, wrap=span)
-    exchanges = (coarse_a, fine_a, coarse_b, fine_b, top_c)
+    def coarse_next(step):
+        return Exchange(16 + 8 * step, c_all, 2 + step, nxc, nyc, 3, 3)
+
+    coarse_a = Exchange(0, c_all, 1, nxc, nyc, 4, 2)
+    fine_a = Exchange(8, f_all, 1, nxf, nyf, 4, 2)
+    fine_b = Exchange(32, f_all, 2, nxf, nyf, 3, 2)
+    exchanges = (coarse_a, fine_a, coarse_next(0), fine_b, coarse_next(1))
 
     for load in loads[0:4]:
         load.wait()
@@ -282,8 +273,8 @@
         @pl.when(jnp.logical_not(exists(-dx, -dy)))
         def _():
             for exchange in exchanges:
-                buffer, where, shape = exchange.targets[n]
-                buffer[where] = jnp.zeros(shape, f32)
+                where, shape = exchange.targets[n]
+                exchange.buffer[where] = jnp.zeros(shape, f32)
 
     cells = (nxc + 4) * span
 
@@ -332,73 +323,94 @@
         par[0] = shear * scale
         par[1] = (par[2] + shear) * scale
 
-    def fine_before(u, earlier):
-        before_halo(u, f1.at[3], f_lift, f_base, earlier, f_par[0], table[...], nxf, nyf)
-
-    def coarse_before(u, earlier):
-        before_halo(u, c1.at[3], c_lift, c_base, earlier, c_par[0], table[...], nxc, nyc)
-
-    def fine_after(u, put):
+    f_metric, c_metric = f_all.at[1, 3], c_all.at[1, 3]
+    sub = lax.broadcasted_iota(jnp.int32, (1, OFF, 1), 1)
+
+    def put_in(buffer, slot, where):
+        def put(c, values):
+            buffer[slot, c, where[0], where[1]] = values
+
+        return put
+
+    def march(step, carry):
+        u_f, u_c = f_all.at[step + 1], c_all.at[step + 1]
+        coarse_b = coarse_next(step)
+        before_halo(
+            u_c,
+            c_metric,
+            c_lift,
+            c_base,
+            lambda c: c_all[step, c, c_in[0], c_in[1]],
+            c_par[0],
+            table[...],
+            nxc,
+            nyc,
+        )
+        pl.when(step == 0)(coarse_a.arrive)
         after_halo(
-            u, f1.at[3], f_lift, f_bend, f_base, f_par[0], f_par[1], table[...], nxf, nyf, 1.0, put
+            u_c,
+            c_metric,
+            c_lift,
+            c_bend,
+            c_base,
+            c_par[0],
+            c_par[1],
+            table[...],
+            nxc,
+            nyc,
+            2.0,
+            put_in(c_all, step + 2, c_in),
         )
-
-    def coarse_after(u, put):
+        coarse_b.start()
+        before_halo(
+            u_f,
+            f_metric,
+            f_lift,
+            f_base,
+            lambda c: f_all[step, c, f_in[0], f_in[1]],
+            f_par[0],
+            table[...],
+            nxf,
+            nyf,
+        )
+        pl.when(step == 0)(fine_a.arrive)
+        pl.when(step == 1)(fine_b.arrive)
         after_halo(
-            u, c1.at[3], c_lift, c_bend, c_base, c_par[0], c_par[1], table[...], nxc, nyc, 2.0, put
+            u_f,
+            f_metric,
+            f_lift,
+            f_bend,
+            f_base,
+            f_par[0],
+            f_par[1],
+            table[...],
+            nxf,
+            nyf,
+            1.0,
+            put_in(f_all, step + 2, f_in),
         )
-
-    def put_in(buffer, where):
-        def put(c, values):
-            buffer[c, where[0], where[1]] = values
-
-        return put
-
-    def put_out(buffer):
-        def put(c, values):
-            buffer[c] = values
-
-        return put
-
-    for load in loads[4:8]:
+        coarse_b.arrive()
+        rims = []
+        for c in range(3):
+            after = c_all[step + 2, c, :, OFF + nyc : 2 * OFF + nyc]
+            before = c_all[step + 2, c, :, 0:OFF]
+            rims.append(jnp.where(sub < 2, after, jnp.where(sub >= OFF - 2, before, 0.0)))
+        middle = [c_all[step + 2, c, :, c_in[1]] for c in range(3)]
+        top = jnp.concatenate([tops(rims), tops(middle)], axis=1)
+        parts = [f_all[step + 2, c, f_in[0], f_in[1]] for c in range(3)]
+        for c, values in enumerate(interface(top, parts)):
+            f_all[step + 2, c, f_in[0], f_in[1]] = values
+        pl.when(step == 0)(fine_b.start)
+        return carry
+
+    for load in loads[4:]:
         load.wait()
     parameters(c_par)
-    coarse_before(c1, lambda c: c_old[c])
-    coarse_a.arrive()
-    coarse_after(c1, put_in(c2, c_in))
-    coarse_b.start()
-    for load in loads[8:12]:
-        load.wait()
     parameters(f_par)
-    fine_before(f1, lambda c: f_old[c])
-    for load in loads[12:]:
-        load.wait()
     build_mix()
-    fine_a.arrive()
-    fine_after(f1, put_in(f2, f_in))
-    coarse_b.arrive()
-    sub = lax.broadcasted_iota(jnp.int32, (1, OFF, 1), 1)
-    rims = []
-    for c in range(3):
-        after, before = c2[c, :, OFF + nyc : 2 * OFF + nyc], c2[c, :, 0:OFF]
-        rims.append(jnp.where(sub < 2, after, jnp.where(sub >= OFF - 2, before, 0.0)))
-    top = jnp.concatenate([tops(rims), tops([c2[c, :, c_in[1]] for c in range(3)])], axis=1)
-    for c, values in enumerate(interface(top, [f2[c, f_in[0], f_in[1]] for c in range(3)])):
-        f2[c, f_in[0], f_in[1]] = values
-    fine_b.start()
-
-    coarse_before(c2, lambda c: c1[c, c_in[0], c_in[1]])
-    coarse_after(c2, put_out(coarse_out))
-    t2[c_in[0], c_in[1]] = tops([coarse_out[c] for c in range(3)])
-    top_c.start()
-    fine_before(f2, lambda c: f1[c, f_in[0], f_in[1]])
-    fine_b.arrive()
-    fine_after(f2, put_out(fine_out))
-    top_c.arrive()
-    rim = jnp.where(jnp.logical_or(sub < 2, sub >= OFF - 2), t2[:, 0:OFF], 0.0)
-    top = jnp.concatenate([rim, t2[:, OFF:span]], axis=1)
-    for c, values in enumerate(interface(top, [fine_out[c] for c in range(3)])):
-        fine_out[c] = values
+    lax.fori_loop(0, 2, march, 0)
+    coarse_out[...] = c_all[3, 0:3, c_in[0], c_in[1]]
+    fine_out[...] = f_all[3, 0:3, f_in[0], f_in[1]]
     for exchange in exchanges:
         exchange.finish()
 
@@ -423,17 +435,13 @@
         _, nxc, nyc, _ = coarse.shape
         index = args[12]
 
-        def wide(parts, nx, ny):
-            return pltpu.VMEM((parts, nx + 4, ny + 2 * OFF, layers), f32)
+        def wide(nx, ny):
+            return pltpu.VMEM((4, 4, nx + 4, ny + 2 * OFF, layers), f32)
 
         span = OFF + nyc
         scratch = [
-            wide(4, nxf, nyf),
-            wide(3, nxf, nyf),
-            wide(4, nxc, nyc),
-            wide(3, nxc, nyc),
-            pltpu.VMEM(fine.shape, f32),
-            pltpu.VMEM(coarse.shape, f32),
+            wide(nxf, nyf),
+            wide(nxc, nyc),
             pltpu.VMEM(fine.shape, f32),
             pltpu.VMEM(coarse.shape, f32),
             pltpu.VMEM(index.shape, jnp.int32),
@@ -442,7 +450,6 @@
             pltpu.VMEM((nxf, nyf + 2 * OFF, layers), f32),
             pltpu.VMEM((nxc + 4, nyc + 2 * OFF, layers), f32),
             pltpu.VMEM((nxc, nyc + 2 * OFF, layers), f32),
-            pltpu.VMEM((nxc + 4, span, layers), f32),
             pltpu.VMEM((2, nxf * nyf, (nxc + 4) * span), bf16),
             pltpu.VMEM((2 * layers, layers), bf16),
             pltpu.VMEM(fine.shape, f32),

time: 17 us -> 17.3 us (1.018)
  Pallas kernels: 16.2 us -> 16.5 us
    pallas_call x1, Pallas kernels: 15.5 us -> 15.8 us  [on_device(): pl.pallas_call(functools.partial(kernel, size_x, size_y), out_shape=(pltp...]
where the time goes in v2:
time: 17.3 us; the launch traced here: 17.2 us
  Pallas kernels  16.5 us (95%)
  between operations  0.64 us (4%)
    pallas_call x1, Pallas kernels, on_device(): pl.pallas_call(functools.partial(kernel, size_x, size_y), out_shape=(pltp...  15.8 us
    pallas_call x1, Pallas kernels, on_device(): pl.pallas_call(finish, out_shape=shapes, in_specs=[vmem, vmem], out_specs...  0.7 us

profile of v2, /device:TPU:3, one launch (start us, length us, event | category | flops | bytes accessed | tf_op | source)
XLA Modules:
  0.0 17.2 jit_solution(6982608079205324751)
XLA Ops:
  0.6 15.8 %shard_map.149 = (f32[3,8,16,128]{3,2,1,0:T(8,128)S(1)}, f32[3,4,8,128]{3,2,1,0:T(8,128)S(1)}) custom-call(f32[3,8,16,128]{3,2,1,0:T(8,128)} %fine_now.1, f32[3,8,16,128]{3,2,1,0:T(8,128)} %fine_prev.1, f32[3,4,8,128]{3,2,1,0:T(8,128)} %coarse_now.1, f32[3,4,8,128]{3,2,1,0:T(8,128)} %coarse_prev.1, f32[8,16,128]{2,1,0:T(8,128)} %fine_rho.1, ...), custom_call_target="tpu_custom_call" | custom-call | tf_op jit(solution)/shard_map/pallas_call | solution.py:467
  16.5 0.7 %shard_map.150 = (f32[3,8,16,128]{3,2,1,0:T(8,128)}, f32[3,4,8,128]{3,2,1,0:T(8,128)}) custom-call(f32[3,8,16,128]{3,2,1,0:T(8,128)S(1)} %get-tuple-element.4.fine_in, f32[3,4,8,128]{3,2,1,0:T(8,128)S(1)} %get-tuple-element.5.coarse_in), custom_call_target="tpu_custom_call" | custom-call | tf_op jit(solution)/shard_map/pallas_call | solution.py:477

commit v3 on v1

--- a/solution.py
+++ b/solution.py
@@ -212,11 +212,8 @@
         pltpu.make_async_copy(source, target, load_sem.at[n])
         for n, (source, target) in enumerate(pairs)
     ]
-    for load in loads:
+    for load in loads[0:4]:
         load.start()
-
-    half = vertical_table12(layers)
-    table[...] = jnp.concatenate([half, half], axis=0)
 
     def source_range(step, start, length):
         return {-1: pl.ds(start, 2), 1: pl.ds(start + length - 2, 2), 0: pl.ds(start, length)}[step]
@@ -226,7 +223,7 @@
         return {-1: pl.ds(after, 2), 1: pl.ds(start - 2, 2), 0: pl.ds(start, length)}[step]
 
     class Exchange:
-        def __init__(self, base, buffer, nx, ny, sides, corners, wrap=0):
+        def __init__(self, base, buffer, nx, ny, sides, corners, wrap=0, operand=None):
             self.copies = []
             self.targets = []
             for n, (dx, dy) in enumerate(DIRS):
@@ -237,9 +234,13 @@
                     src, dst = buffer.at[xs, ys], buffer.at[xt, yt]
                     self.targets.append((buffer, (xt, yt), (xt.size, yt.size, layers)))
                 else:
-                    ps = pl.ds(0, parts)
+                    ps = parts if isinstance(parts, int) else pl.ds(*parts)
                     src, dst = buffer.at[ps, xs, ys], buffer.at[ps, xt, yt]
-                    self.targets.append((buffer, (ps, xt, yt), (parts, xt.size, yt.size, layers)))
+                    lead = () if isinstance(parts, int) else (parts[1],)
+                    self.targets.append((buffer, (ps, xt, yt), lead + (xt.size, yt.size, layers)))
+                    if operand is not None:
+                        xo, yo = source_range(dx, 0, nx), source_range(dy, 0, ny)
+                        src = operand.at[xo, yo] if isinstance(parts, int) else operand.at[ps, xo, yo]
                 copy = pltpu.make_async_remote_copy(
                     src_ref=src,
                     dst_ref=dst,
@@ -250,32 +251,40 @@
                 )
                 self.copies.append(copy)
 
-        def start(self):
-            for n in (4, 5, 6, 7, 0, 1, 2, 3):
+        def start(self, which=(4, 5, 6, 7, 0, 1, 2, 3)):
+            for n in which:
                 pl.when(exists(*DIRS[n]))(self.copies[n].start)
 
-        def arrive(self):
-            for (dx, dy), copy in zip(DIRS, self.copies):
-                pl.when(exists(-dx, -dy))(copy.wait_recv)
-
-        def finish(self):
-            for (dx, dy), copy in zip(DIRS, self.copies):
-                pl.when(exists(dx, dy))(copy.wait_send)
-
-    coarse_a = Exchange(0, c1, nxc, nyc, 4, 2)
-    fine_a = Exchange(8, f1, nxf, nyf, 4, 2)
-    coarse_b = Exchange(16, c2, nxc, nyc, 3, 3)
-    fine_b = Exchange(24, f2, nxf, nyf, 3, 2)
+        def arrive(self, which=range(8)):
+            for n in which:
+                dx, dy = DIRS[n]
+                pl.when(exists(-dx, -dy))(self.copies[n].wait_recv)
+
+        def finish(self, which=range(8)):
+            for n in which:
+                pl.when(exists(*DIRS[n]))(self.copies[n].wait_send)
+
+    whole, pair, sides = (0, 3), (0, 2), range(4)
+    coarse_a = Exchange(0, c1, nxc, nyc, whole, pair, operand=coarse_now)
+    fine_a = Exchange(8, f1, nxf, nyf, whole, pair, operand=fine_now)
+    coarse_b = Exchange(16, c2, nxc, nyc, whole, whole)
+    fine_b = Exchange(24, f2, nxf, nyf, whole, pair)
     top_c = Exchange(32, t2, nxc, nyc, None, None, wrap=span)
-    exchanges = (coarse_a, fine_a, coarse_b, fine_b, top_c)
-
-    for load in loads[0:4]:
-        load.wait()
+    coarse_m = Exchange(40, c1, nxc, nyc, 3, 3, operand=coarse_metric)
+    fine_m = Exchange(48, f1, nxf, nyf, 3, 3, operand=fine_metric)
+    exchanges = (coarse_a, fine_a, coarse_b, fine_b, top_c, coarse_m, fine_m)
+
     sides_x = 1 + (gx >= 1).astype(jnp.int32) + (gx <= size_x - 2).astype(jnp.int32)
     sides_y = 1 + (gy >= 1).astype(jnp.int32) + (gy <= size_y - 2).astype(jnp.int32)
     pl.semaphore_wait(barrier, sides_x * sides_y - 1)
     coarse_a.start()
+    coarse_m.start(sides)
     fine_a.start()
+    fine_m.start(sides)
+    for load in loads[4:]:
+        load.start()
+    half = vertical_table12(layers)
+    table[...] = jnp.concatenate([half, half], axis=0)
 
     for n, (dx, dy) in enumerate(DIRS):
 
@@ -360,22 +369,27 @@
 
         return put
 
-    for load in loads[4:8]:
+    for load in (loads[0], loads[1], *loads[4:8]):
         load.wait()
     parameters(c_par)
     coarse_before(c1, lambda c: c_old[c])
-    coarse_a.arrive()
-    coarse_after(c1, put_in(c2, c_in))
-    coarse_b.start()
-    for load in loads[8:12]:
+    for load in (loads[2], loads[3], *loads[8:12]):
         load.wait()
     parameters(f_par)
     fine_before(f1, lambda c: f_old[c])
+    coarse_a.arrive()
+    coarse_m.arrive(sides)
+    coarse_after(c1, put_in(c2, c_in))
+    coarse_b.start()
+    fine_a.arrive()
+    fine_m.arrive(sides)
+    fine_after(f1, put_in(f2, f_in))
     for load in loads[12:]:
         load.wait()
     build_mix()
-    fine_a.arrive()
-    fine_after(f1, put_in(f2, f_in))
+    coarse_before(c2, lambda c: c1[c, c_in[0], c_in[1]])
+    for exchange, which in ((coarse_a, range(8)), (fine_a, range(8)), (coarse_m, sides), (fine_m, sides)):
+        exchange.finish(which)
     coarse_b.arrive()
     sub = lax.broadcasted_iota(jnp.int32, (1, OFF, 1), 1)
     rims = []
@@ -387,20 +401,20 @@
         f2[c, f_in[0], f_in[1]] = values
     fine_b.start()
 
-    coarse_before(c2, lambda c: c1[c, c_in[0], c_in[1]])
     coarse_after(c2, put_out(coarse_out))
     t2[c_in[0], c_in[1]] = tops([coarse_out[c] for c in range(3)])
     top_c.start()
     fine_before(f2, lambda c: f1[c, f_in[0], f_in[1]])
+    coarse_b.finish()
     fine_b.arrive()
     fine_after(f2, put_out(fine_out))
+    fine_b.finish()
     top_c.arrive()
     rim = jnp.where(jnp.logical_or(sub < 2, sub >= OFF - 2), t2[:, 0:OFF], 0.0)
     top = jnp.concatenate([rim, t2[:, OFF:span]], axis=1)
     for c, values in enumerate(interface(top, [fine_out[c] for c in range(3)])):
         fine_out[c] = values
-    for exchange in exchanges:
-        exchange.finish()
+    top_c.finish()
 
 
 def finish(fine_in, coarse_in, fine_out, coarse_out, sem):
@@ -448,8 +462,8 @@
             pltpu.VMEM(fine.shape, f32),
             pltpu.VMEM(coarse.shape, f32),
             pltpu.SemaphoreType.DMA((14,)),
-            pltpu.SemaphoreType.DMA((40,)),
-            pltpu.SemaphoreType.DMA((40,)),
+            pltpu.SemaphoreType.DMA((56,)),
+            pltpu.SemaphoreType.DMA((56,)),
         ]
         shapes = (
             jax.ShapeDtypeStruct(fine.shape, f32),

time: 17 us -> 17.5 us (1.029)
  Pallas kernels: 16.2 us -> 16.5 us
    pallas_call x1, Pallas kernels: 15.5 us -> 15.8 us  [on_device(): pl.pallas_call(functools.partial(kernel, size_x, size_y), out_shape=(pltp...]
where the time goes in v3:
time: 17.5 us; the launch traced here: 17.2 us
  Pallas kernels  16.5 us (94%)
  between operations  0.64 us (4%)
    pallas_call x1, Pallas kernels, on_device(): pl.pallas_call(functools.partial(kernel, size_x, size_y), out_shape=(pltp...  15.8 us
    pallas_call x1, Pallas kernels, on_device(): pl.pallas_call(finish, out_shape=shapes, in_specs=[vmem, vmem], out_specs...  0.7 us

profile of v3, /device:TPU:3, one launch (start us, length us, event | category | flops | bytes accessed | tf_op | source)
XLA Modules:
  0.0 17.2 jit_solution(12650093498362810517)
XLA Ops:
  0.6 15.8 %shard_map.149 = (f32[3,8,16,128]{3,2,1,0:T(8,128)S(1)}, f32[3,4,8,128]{3,2,1,0:T(8,128)S(1)}) custom-call(f32[3,8,16,128]{3,2,1,0:T(8,128)} %fine_now.1, f32[3,8,16,128]{3,2,1,0:T(8,128)} %fine_prev.1, f32[3,4,8,128]{3,2,1,0:T(8,128)} %coarse_now.1, f32[3,4,8,128]{3,2,1,0:T(8,128)} %coarse_prev.1, f32[8,16,128]{2,1,0:T(8,128)} %fine_rho.1, ...), custom_call_target="tpu_custom_call" | custom-call | tf_op jit(solution)/shard_map/pallas_call | solution.py:474
  16.5 0.7 %shard_map.150 = (f32[3,8,16,128]{3,2,1,0:T(8,128)}, f32[3,4,8,128]{3,2,1,0:T(8,128)}) custom-call(f32[3,8,16,128]{3,2,1,0:T(8,128)S(1)} %get-tuple-element.4.fine_in, f32[3,4,8,128]{3,2,1,0:T(8,128)S(1)} %get-tuple-element.5.coarse_in), custom_call_target="tpu_custom_call" | custom-call | tf_op jit(solution)/shard_map/pallas_call | solution.py:484

commit v4 on v1

--- a/solution.py
+++ b/solution.py
@@ -59,30 +59,30 @@
 def before_halo(u, metric, lift, base, earlier, shear, table2, nx, ny):
     inner_x, inner_y = slice(2, 2 + nx), slice(OFF, OFF + ny)
     metric_in = metric[inner_x, inner_y] * (1.0 / 12.0)
-    present = u[0:3, inner_x, inner_y]
-    slopes = metric_in * vertical12(present, table2)
+    slopes = [metric_in * vertical12(u[c, inner_x, inner_y], table2) for c in range(3)]
     lift[inner_x, inner_y] = slopes[2]
-    bent = metric_in * vertical12(slopes, table2)
     for c in range(3):
-        base[c] = 2.0 * present[c] - earlier(c) + shear * bent[c]
+        bent = metric_in * vertical12(slopes[c], table2)
+        base[c] = 2.0 * u[c, inner_x, inner_y] - earlier(c) + shear[...] * bent
 
 
 def after_halo(u, metric, lift, bend, base, shear, both, table2, nx, ny, spacing, put):
     inner_x, inner_y = slice(2, 2 + nx), slice(OFF, OFF + ny)
     t1 = 1.0 / (12.0 * spacing)
     t2 = 1.0 / (12.0 * spacing * spacing)
+    taps = (-2, -1, 1, 2)
 
     def first(m2, m1, p1, p2):
-        return t1 * ((m2 - p2) + 8.0 * (p1 - m1))
-
-    def second(m2, m1, mid, p1, p2):
-        return t2 * (16.0 * (m1 + p1) - (m2 + p2) - 30.0 * mid)
-
-    def along_y(read):
-        return [read(slice(OFF + s, OFF + s + ny)) for s in (-2, -1, 0, 1, 2)]
-
-    def along_x(values):
-        return [values[2 + s : 2 + s + nx] for s in (-2, -1, 0, 1, 2)]
+        return t1 * (m2 - p2) + (8.0 * t1) * (p1 - m1)
+
+    def pairs(m2, m1, p1, p2):
+        return m1 + p1, m2 + p2
+
+    def second(near, far, mid, weight):
+        return (16.0 * t2) * near - t2 * far - (weight * t2) * mid
+
+    def shifted(read):
+        return [read(slice(OFF + s, OFF + s + ny)) for s in taps]
 
     layers = u.shape[-1]
     rims = (
@@ -91,36 +91,43 @@
         (inner_x, slice(0, OFF)),
         (inner_x, slice(OFF + ny, 2 * OFF + ny)),
     )
-    rows = [u[2, xs, ys].reshape(-1, layers) for xs, ys in rims]
-    found = vertical12(jnp.concatenate(rows, axis=0), table2)
-    start = 0
-    for (xs, ys), part in zip(rims, rows):
-        scale = metric[xs, ys] * (1.0 / 12.0)
-        lift[xs, ys] = scale * found[start : start + part.shape[0]].reshape(scale.shape)
-        start += part.shape[0]
-
-    m2, m1, mid, p1, p2 = along_x(u[0])
-    bend[...] = first(m2, m1, p1, p2) + lift[inner_x]
-    curve_x0 = second(*[v[:, inner_y] for v in (m2, m1, mid, p1, p2)])
-    slope_x0 = bend[:, inner_y]
-
-    m2, m1, mid, p1, p2 = along_y(lambda ys: u[1, :, ys])
-    slant = first(m2, m1, p1, p2) + lift[:, inner_y]
-    spread = slant[inner_x] + slope_x0 - lift[inner_x, inner_y]
-    bent = (metric[inner_x, inner_y] * (1.0 / 12.0)) * vertical12(spread, table2)
-    curve_y1 = second(*[v[inner_x] for v in (m2, m1, mid, p1, p2)])
-    curve_x1 = second(*along_x(mid))
-    m2, m1, _, p1, p2 = along_x(slant)
-    graddiv_0 = curve_x0 + first(m2, m1, p1, p2)
-    curve_y0 = second(*along_y(lambda ys: u[0, inner_x, ys]))
-    put(0, base[0] + shear * (curve_x0 + curve_y0) + both * graddiv_0)
-
-    m2, m1, mid, p1, p2 = along_y(lambda ys: bend[:, ys])
-    graddiv_1 = curve_y1 + first(m2, m1, p1, p2)
-    put(1, base[1] + shear * (curve_x1 + curve_y1) + both * graddiv_1)
-
-    curve_2 = second(*along_x(u[2, :, inner_y])) + second(*along_y(lambda ys: u[2, inner_x, ys]))
-    put(2, base[2] + shear * curve_2 + both * bent)
+    for xs, ys in rims:
+        lift[xs, ys] = (metric[xs, ys] * (1.0 / 12.0)) * vertical12(u[2, xs, ys], table2)
+
+    slants, sums = [], []
+    for row in range(nx + 4):
+        near_y = shifted(lambda ys: u[1, row, ys])
+        slants.append(first(*near_y) + lift[row, inner_y])
+        sums.append(pairs(*near_y))
+        i = row - 4
+        if i < 0:
+            continue
+        m = i + 2
+        wide = [u[0, m + s] for s in taps]
+        bend[i] = first(*wide) + lift[m]
+        near, far = pairs(*[v[inner_y] for v in wide])
+        mid = u[0, m, inner_y]
+        curve_x = second(near, far, mid, 30.0)
+        near, far = pairs(*shifted(lambda ys: u[0, m, ys]))
+        curve = curve_x + second(near, far, mid, 30.0)
+        graddiv = curve_x + first(*[slants[m + s] for s in taps])
+        put(0, i, base[0, i] + shear[i] * curve + both[i] * graddiv)
+        near, far = sums[m]
+        mid = u[1, m, inner_y]
+        curve_y = second(near, far, mid, 30.0)
+        near, far = pairs(*[u[1, m + s, inner_y] for s in taps])
+        curve = curve_y + second(near, far, mid, 30.0)
+        graddiv = curve_y + first(*shifted(lambda ys: bend[i, ys]))
+        put(1, i, base[1, i] + shear[i] * curve + both[i] * graddiv)
+        near, far = pairs(*[u[2, m + s, inner_y] for s in taps])
+        near_y, far_y = pairs(*shifted(lambda ys: u[2, m, ys]))
+        curve = second(near + near_y, far + far_y, u[2, m, inner_y], 60.0)
+        base[2, i] = base[2, i] + shear[i] * curve
+        base[0, i] = slants[m] + (bend[i, inner_y] - lift[m, inner_y])
+
+    bent = (metric[inner_x, inner_y] * (1.0 / 12.0)) * vertical12(base[0], table2)
+    for i in range(nx):
+        put(2, i, base[2, i] + both[i] * bent[i])
 
 
 def kernel(
@@ -290,19 +297,23 @@
     def build_mix():
         width = nyc + 4
         reciprocal = (2048 + width - 1) // width
-        index = index_in[...].reshape(nxf * nyf, -1)
-        weight = weight_in[...].reshape(nxf * nyf, -1)
-        row = jnp.right_shift(index * reciprocal, 11)
-        column = index - row * width + (OFF - 2)
-        column = jnp.where(column >= span, column - span, column)
-        place = row * span + column
-        cell = lax.broadcasted_iota(jnp.int32, (nxf * nyf, cells), 1)
-        total = jnp.zeros((nxf * nyf, cells), f32)
-        for j in range(index.shape[1]):
-            total += jnp.where(cell == place[:, j : j + 1], weight[:, j : j + 1], 0.0)
-        mix_high, mix_low = halves(total)
-        mix[0] = mix_high
-        mix[1] = mix_low
+        planes = max(1, 32 // nyf)
+        rows = planes * nyf
+        cell = lax.broadcasted_iota(jnp.int32, (rows, cells), 1)
+        for part in range(nxf // planes):
+            here = slice(part * planes, (part + 1) * planes)
+            index = index_in[here].reshape(rows, -1)
+            weight = weight_in[here].reshape(rows, -1)
+            row = jnp.right_shift(index * reciprocal, 11)
+            column = index - row * width + (OFF - 2)
+            column = jnp.where(column >= span, column - span, column)
+            place = row * span + column
+            total = jnp.zeros((rows, cells), f32)
+            for j in range(index.shape[1]):
+                total += jnp.where(cell == place[:, j : j + 1], weight[:, j : j + 1], 0.0)
+            mix_high, mix_low = halves(total)
+            mix[0, part * rows : (part + 1) * rows] = mix_high
+            mix[1, part * rows : (part + 1) * rows] = mix_low
 
     lane = lax.broadcasted_iota(jnp.int32, (1, 1, layers), 2)
 
@@ -333,30 +344,30 @@
         par[1] = (par[2] + shear) * scale
 
     def fine_before(u, earlier):
-        before_halo(u, f1.at[3], f_lift, f_base, earlier, f_par[0], table[...], nxf, nyf)
+        before_halo(u, f1.at[3], f_lift, f_base, earlier, f_par.at[0], table[...], nxf, nyf)
 
     def coarse_before(u, earlier):
-        before_halo(u, c1.at[3], c_lift, c_base, earlier, c_par[0], table[...], nxc, nyc)
+        before_halo(u, c1.at[3], c_lift, c_base, earlier, c_par.at[0], table[...], nxc, nyc)
 
     def fine_after(u, put):
         after_halo(
-            u, f1.at[3], f_lift, f_bend, f_base, f_par[0], f_par[1], table[...], nxf, nyf, 1.0, put
+            u, f1.at[3], f_lift, f_bend, f_base, f_par.at[0], f_par.at[1], table[...], nxf, nyf, 1.0, put
         )
 
     def coarse_after(u, put):
         after_halo(
-            u, c1.at[3], c_lift, c_bend, c_base, c_par[0], c_par[1], table[...], nxc, nyc, 2.0, put
+            u, c1.at[3], c_lift, c_bend, c_base, c_par.at[0], c_par.at[1], table[...], nxc, nyc, 2.0, put
         )
 
     def put_in(buffer, where):
-        def put(c, values):
-            buffer[c, where[0], where[1]] = values
+        def put(c, row, values):
+            buffer[c, where[0].start + row, where[1]] = values
 
         return put
 
     def put_out(buffer):
-        def put(c, values):
-            buffer[c] = values
+        def put(c, row, values):
+            buffer[c, row] = values
 
         return put
 

time: 17 us -> 17 us (level)
  no operation moved by 1% of the time
where the time goes in v4:
time: 17 us; the launch traced here: 16.9 us
  Pallas kernels  16.2 us (95%)
  between operations  0.64 us (4%)
    pallas_call x1, Pallas kernels, on_device(): pl.pallas_call(functools.partial(kernel, size_x, size_y), out_shape=(pltp...  15.5 us
    pallas_call x1, Pallas kernels, on_device(): pl.pallas_call(finish, out_shape=shapes, in_specs=[vmem, vmem], out_specs...  0.7 us

profile of v4, /device:TPU:3, one launch (start us, length us, event | category | flops | bytes accessed | tf_op | source)
XLA Modules:
  0.0 16.9 jit_solution(2639450195432546332)
XLA Ops:
  0.6 15.5 %shard_map.149 = (f32[3,8,16,128]{3,2,1,0:T(8,128)S(1)}, f32[3,4,8,128]{3,2,1,0:T(8,128)S(1)}) custom-call(f32[3,8,16,128]{3,2,1,0:T(8,128)} %fine_now.1, f32[3,8,16,128]{3,2,1,0:T(8,128)} %fine_prev.1, f32[3,4,8,128]{3,2,1,0:T(8,128)} %coarse_now.1, f32[3,4,8,128]{3,2,1,0:T(8,128)} %coarse_prev.1, f32[8,16,128]{2,1,0:T(8,128)} %fine_rho.1, ...), custom_call_target="tpu_custom_call" | custom-call | tf_op jit(solution)/shard_map/pallas_call | solution.py:471
  16.2 0.7 %shard_map.150 = (f32[3,8,16,128]{3,2,1,0:T(8,128)}, f32[3,4,8,128]{3,2,1,0:T(8,128)}) custom-call(f32[3,8,16,128]{3,2,1,0:T(8,128)S(1)} %get-tuple-element.4.fine_in, f32[3,4,8,128]{3,2,1,0:T(8,128)S(1)} %get-tuple-element.5.coarse_in), custom_call_target="tpu_custom_call" | custom-call | tf_op jit(solution)/shard_map/pallas_call | solution.py:481

commit v5 on v4

--- a/solution.py
+++ b/solution.py
@@ -219,11 +219,8 @@
         pltpu.make_async_copy(source, target, load_sem.at[n])
         for n, (source, target) in enumerate(pairs)
     ]
-    for load in loads:
+    for load in loads[0:4]:
         load.start()
-
-    half = vertical_table12(layers)
-    table[...] = jnp.concatenate([half, half], axis=0)
 
     def source_range(step, start, length):
         return {-1: pl.ds(start, 2), 1: pl.ds(start + length - 2, 2), 0: pl.ds(start, length)}[step]
@@ -276,13 +273,19 @@
     top_c = Exchange(32, t2, nxc, nyc, None, None, wrap=span)
     exchanges = (coarse_a, fine_a, coarse_b, fine_b, top_c)
 
-    for load in loads[0:4]:
-        load.wait()
     sides_x = 1 + (gx >= 1).astype(jnp.int32) + (gx <= size_x - 2).astype(jnp.int32)
     sides_y = 1 + (gy >= 1).astype(jnp.int32) + (gy <= size_y - 2).astype(jnp.int32)
+    for load in loads[0:2]:
+        load.wait()
     pl.semaphore_wait(barrier, sides_x * sides_y - 1)
     coarse_a.start()
+    for load in loads[2:4]:
+        load.wait()
     fine_a.start()
+    for load in loads[4:]:
+        load.start()
+    half = vertical_table12(layers)
+    table[...] = jnp.concatenate([half, half], axis=0)
 
     for n, (dx, dy) in enumerate(DIRS):
 
@@ -375,18 +378,21 @@
         load.wait()
     parameters(c_par)
     coarse_before(c1, lambda c: c_old[c])
-    coarse_a.arrive()
-    coarse_after(c1, put_in(c2, c_in))
-    coarse_b.start()
     for load in loads[8:12]:
         load.wait()
     parameters(f_par)
     fine_before(f1, lambda c: f_old[c])
+    coarse_a.arrive()
+    coarse_after(c1, put_in(c2, c_in))
+    coarse_b.start()
+    fine_a.arrive()
+    fine_after(f1, put_in(f2, f_in))
     for load in loads[12:]:
         load.wait()
     build_mix()
-    fine_a.arrive()
-    fine_after(f1, put_in(f2, f_in))
+    coarse_before(c2, lambda c: c1[c, c_in[0], c_in[1]])
+    coarse_a.finish()
+    fine_a.finish()
     coarse_b.arrive()
     sub = lax.broadcasted_iota(jnp.int32, (1, OFF, 1), 1)
     rims = []
@@ -398,20 +404,20 @@
         f2[c, f_in[0], f_in[1]] = values
     fine_b.start()
 
-    coarse_before(c2, lambda c: c1[c, c_in[0], c_in[1]])
     coarse_after(c2, put_out(coarse_out))
     t2[c_in[0], c_in[1]] = tops([coarse_out[c] for c in range(3)])
     top_c.start()
     fine_before(f2, lambda c: f1[c, f_in[0], f_in[1]])
+    coarse_b.finish()
     fine_b.arrive()
     fine_after(f2, put_out(fine_out))
+    fine_b.finish()
     top_c.arrive()
     rim = jnp.where(jnp.logical_or(sub < 2, sub >= OFF - 2), t2[:, 0:OFF], 0.0)
     top = jnp.concatenate([rim, t2[:, OFF:span]], axis=1)
     for c, values in enumerate(interface(top, [fine_out[c] for c in range(3)])):
         fine_out[c] = values
-    for exchange in exchanges:
-        exchange.finish()
+    top_c.finish()
 
 
 def finish(fine_in, coarse_in, fine_out, coarse_out, sem):

time: 17 us -> 16.9 us (level)
    pallas_call x1, Pallas kernels: 15.5 us -> 15.3 us  [on_device(): pl.pallas_call(functools.partial(kernel, size_x, size_y), out_shape=(pltp...]
where the time goes in v5:
time: 16.9 us; the launch traced here: 16.7 us
  Pallas kernels  16.1 us (95%)
  between operations  0.64 us (4%)
    pallas_call x1, Pallas kernels, on_device(): pl.pallas_call(functools.partial(kernel, size_x, size_y), out_shape=(pltp...  15.3 us
    pallas_call x1, Pallas kernels, on_device(): pl.pallas_call(finish, out_shape=shapes, in_specs=[vmem, vmem], out_specs...  0.7 us

profile of v5, /device:TPU:3, one launch (start us, length us, event | category | flops | bytes accessed | tf_op | source)
XLA Modules:
  0.0 16.7 jit_solution(18292589716995602300)
XLA Ops:
  0.6 15.3 %shard_map.149 = (f32[3,8,16,128]{3,2,1,0:T(8,128)S(1)}, f32[3,4,8,128]{3,2,1,0:T(8,128)S(1)}) custom-call(f32[3,8,16,128]{3,2,1,0:T(8,128)} %fine_now.1, f32[3,8,16,128]{3,2,1,0:T(8,128)} %fine_prev.1, f32[3,4,8,128]{3,2,1,0:T(8,128)} %coarse_now.1, f32[3,4,8,128]{3,2,1,0:T(8,128)} %coarse_prev.1, f32[8,16,128]{2,1,0:T(8,128)} %fine_rho.1, ...), custom_call_target="tpu_custom_call" | custom-call | tf_op jit(solution)/shard_map/pallas_call | solution.py:477
  16.0 0.7 %shard_map.150 = (f32[3,8,16,128]{3,2,1,0:T(8,128)}, f32[3,4,8,128]{3,2,1,0:T(8,128)}) custom-call(f32[3,8,16,128]{3,2,1,0:T(8,128)S(1)} %get-tuple-element.4.fine_in, f32[3,4,8,128]{3,2,1,0:T(8,128)S(1)} %get-tuple-element.5.coarse_in), custom_call_target="tpu_custom_call" | custom-call | tf_op jit(solution)/shard_map/pallas_call | solution.py:487

commit v6 on v5

--- a/solution.py
+++ b/solution.py
@@ -255,7 +255,7 @@
                 self.copies.append(copy)
 
         def start(self):
-            for n in (4, 5, 6, 7, 0, 1, 2, 3):
+            for n in (0, 1, 2, 3, 4, 5, 6, 7):
                 pl.when(exists(*DIRS[n]))(self.copies[n].start)
 
         def arrive(self):

time: 16.9 us -> 17.2 us (1.018)
  Pallas kernels: 16.1 us -> 16.4 us
    pallas_call x1, Pallas kernels: 15.3 us -> 15.7 us  [on_device(): pl.pallas_call(functools.partial(kernel, size_x, size_y), out_shape=(pltp...]
where the time goes in v6:
time: 17.2 us; the launch traced here: 17 us
  Pallas kernels  16.4 us (95%)
  between operations  0.64 us (4%)
    pallas_call x1, Pallas kernels, on_device(): pl.pallas_call(functools.partial(kernel, size_x, size_y), out_shape=(pltp...  15.7 us
    pallas_call x1, Pallas kernels, on_device(): pl.pallas_call(finish, out_shape=shapes, in_specs=[vmem, vmem], out_specs...  0.7 us

profile of v6, /device:TPU:3, one launch (start us, length us, event | category | flops | bytes accessed | tf_op | source)
XLA Modules:
  0.0 17.0 jit_solution(1467167586948491676)
XLA Ops:
  0.6 15.7 %shard_map.149 = (f32[3,8,16,128]{3,2,1,0:T(8,128)S(1)}, f32[3,4,8,128]{3,2,1,0:T(8,128)S(1)}) custom-call(f32[3,8,16,128]{3,2,1,0:T(8,128)} %fine_now.1, f32[3,8,16,128]{3,2,1,0:T(8,128)} %fine_prev.1, f32[3,4,8,128]{3,2,1,0:T(8,128)} %coarse_now.1, f32[3,4,8,128]{3,2,1,0:T(8,128)} %coarse_prev.1, f32[8,16,128]{2,1,0:T(8,128)} %fine_rho.1, ...), custom_call_target="tpu_custom_call" | custom-call | tf_op jit(solution)/shard_map/pallas_call | solution.py:477
  16.3 0.7 %shard_map.150 = (f32[3,8,16,128]{3,2,1,0:T(8,128)}, f32[3,4,8,128]{3,2,1,0:T(8,128)}) custom-call(f32[3,8,16,128]{3,2,1,0:T(8,128)S(1)} %get-tuple-element.4.fine_in, f32[3,4,8,128]{3,2,1,0:T(8,128)S(1)} %get-tuple-element.5.coarse_in), custom_call_target="tpu_custom_call" | custom-call | tf_op jit(solution)/shard_map/pallas_call | solution.py:487
